TPU v7x, 256 devices: a whole 4x4x8 slice. The times are simulated.
256 devices in a mesh: seq: 16 (over z, x_lo), res: 16 (over x_hi, y, core).
Axes of the slice: x: 4 (x_hi: 2, x_lo: 2; x = x_hi * 2 + x_lo), y: 4, z: 8, core: 2. Of those that a mesh axis runs over, the one named last changes fastest.
Arguments:
- homolog_embedding: bfloat16 [160, 2048, 256], P('seq', 'res'), may hold values from -6 to 6
- contact_embedding: bfloat16 [2048, 2048, 128], P('seq', 'res'), may hold values from -6 to 6
- homolog_scaling_factor: float32 [256], replicated, may hold values from 0.5 to 12
- homolog_centering_shift: float32 [256], replicated, may hold values from -3 to 3
- contact_scaling_factor: float32 [128], replicated, may hold values from 0.1 to 1.9
- asking_projection_matrix: bfloat16 [256, 256], replicated, may hold values from -0.375 to 0.375
- lookup_projection_matrix: bfloat16 [256, 256], replicated, may hold values from -0.375 to 0.375
- content_projection_matrix: bfloat16 [256, 256], replicated, may hold values from -0.375 to 0.375
- sigmoid_projection_matrix: bfloat16 [256, 256], replicated, may hold values from -0.375 to 0.375
- sigmoid_shift_term: float32 [256], replicated, may hold values from -4 to 4
- contact_logit_projection: bfloat16 [128, 8], replicated, may hold values from -0.5 to 0.5
- final_projection_matrix: bfloat16 [256, 256], replicated, may hold values from -0.375 to 0.375
Outputs:
- update: bfloat16 [160, 2048, 256], P('seq', 'res')
All inputs are finite; a program needn't handle non-finite values.
Results may differ from a plain program's by a relative error of at most 0.0075.
The roundings to bfloat16 on the way count: a program that leaves them out, or rounds other values in their place, can miss the bound.
Values may be sent and summed in bfloat16 or wider, within the bound.
A program may use at most 128 MiB of HBM per device.

v0:
```python
import math

import jax
import jax.numpy as jnp
from jax import lax
from jax.sharding import PartitionSpec as P

H = 8
HD = 32


def standardize_channels(values, gain, shift):
    mean = jnp.mean(values, axis=-1, keepdims=True)
    centered = values - mean
    var = jnp.mean(centered * centered, axis=-1, keepdims=True)
    return centered * lax.rsqrt(var + 1e-05) * gain + shift


def local(
    homolog_embedding,
    contact_embedding,
    homolog_scaling_factor,
    homolog_centering_shift,
    contact_scaling_factor,
    asking_projection_matrix,
    lookup_projection_matrix,
    content_projection_matrix,
    sigmoid_projection_matrix,
    sigmoid_shift_term,
    contact_logit_projection,
    final_projection_matrix,
):
    homolog_strip_entries, amino_strip_entries, channel_dimension = homolog_embedding.shape
    homolog_standardized = standardize_channels(
        homolog_embedding.astype(jnp.float32), homolog_scaling_factor, homolog_centering_shift
    ).astype(jnp.bfloat16)
    flat = homolog_standardized.reshape(
        homolog_strip_entries * amino_strip_entries, channel_dimension
    )
    query = (
        (jnp.dot(flat, asking_projection_matrix, preferred_element_type=jnp.float32) * HD ** (-0.5))
        .astype(jnp.bfloat16)
        .reshape(homolog_strip_entries, amino_strip_entries, H, HD)
    )
    gate = jax.nn.sigmoid(
        jnp.dot(flat, sigmoid_projection_matrix, preferred_element_type=jnp.float32)
        + sigmoid_shift_term
    ).reshape(homolog_strip_entries, amino_strip_entries, channel_dimension)
    pair_rows, pair_cols, pair_width = contact_embedding.shape
    normed_pair = standardize_channels(
        contact_embedding.astype(jnp.float32), contact_scaling_factor, 0.0
    ).astype(jnp.bfloat16)
    tile = jnp.dot(
        normed_pair.reshape(pair_rows * pair_cols, pair_width),
        contact_logit_projection,
        preferred_element_type=jnp.float32,
    )
    tile = tile.astype(jnp.bfloat16).reshape(pair_rows, pair_cols, H).transpose(2, 0, 1)
    columns = lax.all_gather(tile, "seq", axis=1, tiled=True)
    bias_local = lax.all_to_all(columns, "res", split_axis=1, concat_axis=2, tiled=True)
    init = (
        jnp.full((homolog_strip_entries, H, amino_strip_entries), -1e30, jnp.float32),
        jnp.zeros((homolog_strip_entries, H, amino_strip_entries), jnp.float32),
        jnp.zeros((homolog_strip_entries, H, amino_strip_entries, HD), jnp.float32),
    )
    key_local = (
        jnp.dot(flat, lookup_projection_matrix, preferred_element_type=jnp.float32)
        .astype(jnp.bfloat16)
        .reshape(homolog_strip_entries, amino_strip_entries, H, HD)
    )
    value_local = (
        jnp.dot(flat, content_projection_matrix, preferred_element_type=jnp.float32)
        .astype(jnp.bfloat16)
        .reshape(homolog_strip_entries, amino_strip_entries, H, HD)
    )
    keys = lax.all_gather(key_local, "res", axis=1, tiled=True)
    values = lax.all_gather(value_local, "res", axis=1, tiled=True)
    count = keys.shape[1]
    block = math.gcd(count, 256)

    def step(index, state):
        run_max, total, acc = state
        offset = (index * block).astype(jnp.int32)
        key_block = lax.dynamic_slice_in_dim(keys, offset, block, 1)
        value_block = lax.dynamic_slice_in_dim(values, offset, block, 1)
        bias_block = lax.dynamic_slice_in_dim(bias_local, offset, block, 2)
        scores = jnp.einsum("sqhd,skhd->shqk", query, key_block, preferred_element_type=jnp.float32)
        scores = scores + bias_block.astype(jnp.float32)[None]
        new_max = jnp.maximum(run_max, jnp.max(scores, axis=-1))
        factor = jnp.exp(run_max - new_max)
        weights = jnp.exp(scores - new_max[..., None])
        total = total * factor + jnp.sum(weights, axis=-1)
        acc = acc * factor[..., None] + jnp.einsum(
            "shqk,skhd->shqd",
            weights.astype(jnp.bfloat16),
            value_block,
            preferred_element_type=jnp.float32,
        )
        return (new_max, total, acc)

    result = lax.fori_loop(0, count // block, step, init)
    run_max, total, acc = result
    attended = (
        (acc / total[..., None])
        .transpose(0, 2, 1, 3)
        .reshape(homolog_strip_entries, amino_strip_entries, channel_dimension)
    )
    gated = (gate * attended).astype(jnp.bfloat16)
    update = jnp.dot(
        gated.reshape(homolog_strip_entries * amino_strip_entries, channel_dimension),
        final_projection_matrix,
        preferred_element_type=jnp.float32,
    )
    return update.astype(jnp.bfloat16).reshape(
        homolog_strip_entries, amino_strip_entries, channel_dimension
    )


def solution(mesh):
    in_specs = (
        P("seq", "res", None),
        P("seq", "res", None),
        P(),
        P(),
        P(),
        P(),
        P(),
        P(),
        P(),
        P(),
        P(),
        P(),
    )
    out_specs = P("seq", "res", None)
    return jax.shard_map(local, mesh=mesh, in_specs=in_specs, out_specs=out_specs, check_vma=False)
```

profile of v0, /device:TPU:128, one launch (start us, length us, event | category | flops | bytes accessed | tf_op | source)
XLA Modules:
  0.0 518.8 jit_solution(17725393256473855245)
XLA Ops:
  6.5 3.5 convert_reduce_fusion
  10.1 4.8 fusion.18
  14.9 4.9 fusion.20
  27.1 94.8 %all-gather.6.cloned.1.call-done = bf16[8,2048,128]{2,0,1:T(8,128)(2,1)} async-done(((bf16[8,128,128]{2,0,1:T(8,128)(2,1)}), bf16[8,2048,128]{2,0,1:T(8,128)(2,1)}) %all-gather.6.cloned.1.call-update) | async-done | bytes 4194320 | tf_op jit(solution)/shard_map/all_gather | solution.py:59
  121.9 6.2 %all-to-all-start = ((bf16[8,2048,128]{2,0,1:T(8,128)(2,1)}), bf16[8,2048,128]{2,0,1:T(8,128)(2,1)}, u32[]{:S(2)}, u32[]{:S(2)}) async-start(bf16[8,2048,128]{2,0,1:T(8,128)(2,1)} %all-gather.6.cloned.1.call-done), calls=%async_computation | async-start | bytes 8388608 | tf_op jit(solution)/shard_map/all_to_all | solution.py:60
  131.6 59.7 %all-to-all-done = bf16[8,2048,128]{2,0,1:T(8,128)(2,1)} async-done(((bf16[8,2048,128]{2,0,1:T(8,128)(2,1)}), bf16[8,2048,128]{2,0,1:T(8,128)(2,1)}, u32[]{:S(2)}, u32[]{:S(2)}) %all-to-all-start) | async-done | bytes 4194336 | tf_op jit(solution)/shard_map/all_to_all | solution.py:60
  191.3 6.8 %copy.30 = bf16[8,128,16,128]{1,3,2,0:T(8,128)(2,1)} copy(bf16[8,128,16,128]{3,0,1,2:T(8,128)(2,1)} %bitcast.5) | data formatting | bytes 8388608 | tf_op jit(solution)/shard_map/all_to_all | solution.py:60
  198.1 85.0 %all-gather.8.cloned.1.call-done = bf16[10,2048,8,32]{1,0,3,2:T(8,128)(2,1)} async-done(((bf16[10,128,8,32]{1,0,3,2:T(8,128)(2,1)}), bf16[10,2048,8,32]{1,0,3,2:T(8,128)(2,1)}) %all-gather.8.cloned.1.call-update) | async-done | bytes 10485776 | tf_op jit(solution)/shard_map/all_gather | solution.py:77
  283.1 13.4 %copy.34 = bf16[10,2048,8,32]{1,3,2,0:T(8,128)(2,1)} copy(bf16[10,2048,8,32]{1,0,3,2:T(8,128)(2,1)} %all-gather.8.cloned.1.call-done) | data formatting | bytes 20971520
  296.5 110.5 %all-gather.4.cloned.1.call-done = bf16[10,2048,8,32]{1,0,3,2:T(8,128)(2,1)} async-done(((bf16[10,128,8,32]{1,0,3,2:T(8,128)(2,1)}), bf16[10,2048,8,32]{1,0,3,2:T(8,128)(2,1)}) %all-gather.4.cloned.1.call-update) | async-done | bytes 10485776 | tf_op jit(solution)/shard_map/all_gather | solution.py:76
  406.9 13.4 %copy.32 = bf16[10,2048,8,32]{1,3,2,0:T(8,128)(2,1)} copy(bf16[10,2048,8,32]{1,0,3,2:T(8,128)(2,1)} %all-gather.4.cloned.1.call-done) | data formatting | bytes 20971520
  420.4 86.0 %while.18 = (s32[]{:T(128)}, f32[10,8,128]{2,1,0:T(8,128)S(1)}, f32[10,8,128]{2,1,0:T(8,128)S(1)}, f32[10,8,128,32]{2,3,1,0:T(8,128)S(1)}, bf16[10,2048,8,32]{1,...) while((s32[]{:T(128)}, f32[10,8,128]{2,1,0:T(8,128)S(1)}, ...), condition=%wide.region_7.0_spmd.clone, body=%wide.region_4.0_spmd.clone.sunk | while | flops 357812224 | bytes 42729664 | solution.py:101
  421.5 3.2 fusion.60
  424.7 2.7 fusion.61
  427.4 3.7 fusion.63
  432.2 3.2 fusion.60
  438.1 3.7 fusion.63
  443.0 3.2 fusion.60
  448.9 3.7 fusion.63
  453.7 3.2 fusion.60
  456.9 2.7 fusion.61
  459.6 3.7 fusion.63
  464.5 3.2 fusion.60
  467.7 2.7 fusion.61
  470.4 3.7 fusion.63
  475.2 3.2 fusion.60
  481.1 3.7 fusion.63
  486.0 3.2 fusion.60
  491.9 3.7 fusion.63
  496.8 3.2 fusion.60
  502.7 3.7 fusion.63
  509.4 2.8 convolution_convert_fusion.1
  (94 shorter events, 36.2 us)
Async XLA Ops:
  6.5 16.5 %copy-start = (bf16[256,256]{1,0:T(8,128)(2,1)S(1)}, bf16[256,256]{1,0:T(8,128)(2,1)}, u32[]{:S(2)}) copy-start(bf16[256,256]{1,0:T(8,128)(2,1)} %param.21) | copy-start | bytes 393220
  6.5 115.4 %all-gather.6.cloned.1.call-start = ((), (), s32[]{:S(2)}) async-start(), calls=%async_computation.2 | async-start | bytes 4456448 | tf_op jit(solution)/shard_map/all_gather | solution.py:59
  6.5 3.5 copy-start.2
  10.1 4.8 copy-start.9
  14.9 4.9 copy-start.6
  19.8 2.0 copy-start.3
  19.9 2.7 copy-start.7
  19.9 2.7 copy-start.8
  21.8 261.3 %all-gather.8.cloned.1.call-start = ((), (), s32[]{:S(2)}) async-start(), calls=%async_computation.3 | async-start | bytes 17825792 | tf_op jit(solution)/shard_map/all_gather | solution.py:77
  23.4 1.7 copy-start.4
  25.0 381.9 %all-gather.4.cloned.1.call-start = ((), (), s32[]{:S(2)}) async-start(), calls=%async_computation.1 | async-start | bytes 17825792 | tf_op jit(solution)/shard_map/all_gather | solution.py:76
  27.1 101.1 %copy-start.5 = (bf16[256,256]{1,0:T(8,128)(2,1)S(1)}, bf16[256,256]{1,0:T(8,128)(2,1)}, u32[]{:S(2)}) copy-start(bf16[256,256]{1,0:T(8,128)(2,1)} %param.19) | copy-start | bytes 393220
  121.9 69.4 %all-to-all-start = ((bf16[8,2048,128]{2,0,1:T(8,128)(2,1)}), bf16[8,2048,128]{2,0,1:T(8,128)(2,1)}, u32[]{:S(2)}, u32[]{:S(2)}) async-start(bf16[8,2048,128]{2,0,1:T(8,128)(2,1)} %all-gather.6.cloned.1.call-done), calls=%async_computation | async-start | bytes 8388608 | tf_op jit(solution)/shard_map/all_to_all | solution.py:60
  507.9 1.5 copy-start.10
  507.9 1.5 copy-start.11
  507.9 1.5 copy-start.12
  507.9 4.3 copy-start.1
Sparse Core Ops, SparseCore 0:
  21.9 99.9 all-gather.5
  124.5 158.5 all-gather.7
  285.6 121.2 all-gather.3
where the time goes:
time: 523 us; the launch traced here: 519 us
  waiting for transfers between devices  350 us (67%)
  matrix products  60.5 us (12%)
  other arithmetic  45.1 us (9%)
  local copies, waits for them, and re-layouts  42.8 us (8%)
  between operations  13.4 us (3%)
  starting transfers between devices  6.32 us (1%)
    all_gather x1, waiting for transfers between devices, local(): keys = lax.all_gather(key_local, 'res', axis=1, tiled=True)  110 us
    all_gather x1, waiting for transfers between devices, local(): columns = lax.all_gather(tile, 'seq', axis=1, tiled=True)  94.8 us
    all_gather x1, waiting for transfers between devices, local(): values = lax.all_gather(value_local, 'res', axis=1, tiled=True)  85 us
    all_to_all x1, waiting for transfers between devices, local(): lax.all_to_all(columns, 'res', split_axis=1, concat_axis=2, tiled=True)  59.7 us
    dot_general x8, matrix products, step(): jnp.einsum('shqk,skhd->shqd', weights.astype(jnp.bfloat16), value_block,...  29.5 us
    unnamed x30, local copies, waits for them, and re-layouts  28.8 us
    dot_general x8, matrix products, step(): jnp.einsum('sqhd,skhd->shqk', query, key_block, preferred_element_type=jn...  25.3 us
    reduce_sum x8, other arithmetic, step(): total = total * factor + jnp.sum(weights, axis=-1)  21.4 us
  transfers between devices with their start and end apart: 4, of which 4 were waited for; matrix products, arithmetic and copies ran while one was open for 6% of the time, Pallas kernels for 0%

commit v1 on v0

v1 whole, which is shorter than its diff:
```python
import functools

import jax
import jax.numpy as jnp
from jax import lax
from jax.experimental import pallas as pl
from jax.experimental.pallas import tpu as pltpu
from jax.sharding import PartitionSpec as P

F32, BF = jnp.float32, jnp.bfloat16
MESH = pl.DeviceIdType.MESH
VMEM = pl.BlockSpec(memory_space=pltpu.VMEM)
HBM = pl.BlockSpec(memory_space=pl.ANY)

H, HD = 8, 32
SEQS, RES, CH, CP = 10, 128, 256, 128
KEYS = 2048
ROWS = SEQS * HD
PAIRS = SEQS // 2
TILE = 256
LIMIT = 56 * 2**20


def normalize(values, gain):
    mean = jnp.mean(values, axis=-1, keepdims=True)
    centered = values - mean
    var = jnp.mean(centered * centered, axis=-1, keepdims=True)
    return centered * lax.rsqrt(var + 1e-05) * gain


def pair_kernel(steps, x_ref, gain_ref, w_ref, o_ref, scr):
    step = pl.program_id(0)
    n = x_ref.shape[0]
    x = x_ref[...].reshape(n * RES, CP).astype(F32)
    pn = normalize(x, gain_ref[...]).astype(BF)
    out = lax.dot_general(w_ref[...], pn, (((1,), (1,)), ((), ())), preferred_element_type=F32)
    for i in range(n):
        row = pl.multiple_of((step * n + i) * H, H)
        scr[pl.ds(row, H), :] = out[:, i * RES : (i + 1) * RES]

    @pl.when(step == steps - 1)
    def _():
        for h in range(H):
            o_ref[h] = scr[pl.ds(h, RES, stride=H), :].T.astype(BF)


def pair_bias(contact, gain, w):
    n = 16
    steps = RES // n
    return pl.pallas_call(
        functools.partial(pair_kernel, steps),
        name="pair_bias",
        grid=(steps,),
        out_shape=jax.ShapeDtypeStruct((H, RES, RES), BF),
        in_specs=[
            pl.BlockSpec((n, RES, CP), lambda i: (i, 0, 0)),
            pl.BlockSpec((1, CP), lambda i: (0, 0)),
            pl.BlockSpec((H, CP), lambda i: (0, 0)),
        ],
        out_specs=pl.BlockSpec((H, RES, RES), lambda i: (0, 0, 0)),
        scratch_shapes=[pltpu.VMEM((RES * H, RES), F32)],
    )(contact, gain.reshape(1, CP), w.T)


def proj_kernel(x_ref, gain_ref, shift_ref, wk_ref, wv_ref, wq_ref, wg_ref, gs_ref, qkv_ref, gate_ref):
    wt = [w[...].astype(F32).T.astype(BF) for w in (wk_ref, wv_ref, wq_ref, wg_ref)]
    nt = (((1,), (1,)), ((), ()))
    for p in range(PAIRS):
        x = x_ref[2 * p : 2 * p + 2].reshape(2 * RES, CH).astype(F32)
        normed = (normalize(x, gain_ref[...]) + shift_ref[...]).astype(BF)
        for j in range(3):
            y = lax.dot_general(wt[j], normed, nt, preferred_element_type=F32)
            if j == 2:
                y = y * HD ** (-0.5)
            y = y.astype(BF)
            for h in range(H):
                for s in range(2):
                    qkv_ref[h, j, (2 * p + s) * HD : (2 * p + s + 1) * HD, :] = y[
                        h * HD : (h + 1) * HD, s * RES : (s + 1) * RES
                    ]
        g = jax.nn.sigmoid(
            lax.dot_general(wt[3], normed, nt, preferred_element_type=F32) + gs_ref[...]
        )
        gate_ref[2 * p] = g[:, :RES]
        gate_ref[2 * p + 1] = g[:, RES:]


def projections(x, gain, shift, wk, wv, wq, wg, gs):
    return pl.pallas_call(
        proj_kernel,
        name="projections",
        out_shape=(
            jax.ShapeDtypeStruct((H, 3, ROWS, RES), BF),
            jax.ShapeDtypeStruct((SEQS, CH, RES), F32),
        ),
        in_specs=[VMEM] * 8,
        out_specs=(VMEM, VMEM),
        compiler_params=pltpu.CompilerParams(vmem_limit_bytes=LIMIT),
    )(x, gain.reshape(1, CH), shift.reshape(1, CH), wk, wv, wq, wg, gs.reshape(CH, 1))


def aligned(value, n):
    return pl.multiple_of(value, n)


def attention_kernel(
    qkv, tiles, out,
    kt, vt, qt, bias, kn, sa, sb, o,
    tile_send, lo_send, kvq_send, core_send, ring_send, out_send,
    bias_recv, kvq_recv, core_recv, ring_recv, out_recv, local_sem,
):
    seq, res = lax.axis_index("seq"), lax.axis_index("res")
    z, low = seq // 2, lax.rem(seq, 2)
    chip, core = res // 2, lax.rem(res, 2)
    owner = core == low

    def at(other_chip, other_core):
        return (seq, other_chip * 2 + other_core)

    def along_z(d):
        return (lax.rem(z + d + 8, 8) * 2 + low, res)

    sibling = at(chip, 1 - core)
    across = (z * 2 + 1 - low, res)

    def remote(src, dst, send, recv, device):
        return pltpu.make_async_remote_copy(
            src_ref=src, dst_ref=dst, send_sem=send, recv_sem=recv, device_id=device, device_id_type=MESH
        )

    def wait_bytes(ref, sem):
        pltpu.make_async_copy(ref, ref, sem).wait()

    barrier = pltpu.get_barrier_semaphore()
    for d in range(1, 16):
        pl.semaphore_signal(barrier, inc=1, device_id=(seq, lax.rem(res + d, 16)), device_id_type=MESH)
    for peer in (across, along_z(1), along_z(-1)):
        pl.semaphore_signal(barrier, inc=1, device_id=peer, device_id_type=MESH)
    pl.semaphore_wait(barrier, 18)

    mine = pl.ds(aligned(core * 1024 + chip * RES, RES), RES)

    def tile_copy(d):
        to = lax.rem(chip + d, 8)
        return remote(tiles.at[to], bias.at[z, mine, :], tile_send.at[d], bias_recv, at(to, low))

    tile_local = pltpu.make_async_copy(tiles.at[chip], bias.at[z, mine, :], bias_recv)
    for d in range(1, 8):
        tile_copy(d).start()

    @pl.when(owner)
    def _():
        tile_local.start()

    @pl.when(jnp.logical_not(owner))
    def _():
        tile_copy(0).start()

    def kvq_copies(d):
        to = lax.rem(chip + d, 8)
        dsts = (kt.at[:, mine], vt.at[:, mine], qt.at[chip])
        return [
            remote(qkv.at[to, j], dsts[j], kvq_send.at[d, j], kvq_recv.at[j], at(to, core)) for j in range(3)
        ]

    for j, dst in enumerate((kt.at[:, mine], vt.at[:, mine], qt.at[chip])):
        pltpu.make_async_copy(qkv.at[chip, j], dst, kvq_recv.at[j]).start()
    for d in range(1, 8):
        for c in kvq_copies(d):
            c.start()

    def ring_copy(sign, k):
        chunk = lax.rem(z - sign * (k - 1) + 8, 8)
        ref = bias.at[chunk]
        if k == 4:
            ref = bias.at[chunk, pl.ds(0 if sign > 0 else KEYS // 2, KEYS // 2), :]
        i = 0 if sign > 0 else 1
        return remote(ref, ref, ring_send.at[i, k - 1], ring_recv.at[i, k - 1], along_z(sign))

    def ring_arrived(sign, k):
        chunk = lax.rem(z - sign * k + 8, 8)
        ref = bias.at[chunk]
        if k == 4:
            ref = bias.at[chunk, pl.ds(0 if sign > 0 else KEYS // 2, KEYS // 2), :]
        wait_bytes(ref, ring_recv.at[0 if sign > 0 else 1, k - 1])

    wait_bytes(bias.at[z], bias_recv)
    lo_copy = remote(bias.at[z], bias.at[z], lo_send, bias_recv, across)

    @pl.when(owner)
    def _():
        lo_copy.start()

    ring_copy(1, 1).start()
    ring_copy(-1, 1).start()

    ring_arrived(1, 1)
    ring_copy(1, 2).start()
    ring_arrived(-1, 1)
    ring_copy(-1, 2).start()

    here = pl.ds(aligned(core * 1024, 1024), 1024)
    there = pl.ds(aligned((1 - core) * 1024, 1024), 1024)
    passed = []
    for j, ref in enumerate((kt, vt)):
        wait_bytes(ref.at[:, here], kvq_recv.at[j])
        c = remote(ref.at[:, here], ref.at[:, here], core_send.at[j], core_recv.at[j], sibling)
        c.start()
        passed.append(c)

    def turn_keys(half):
        for b in range(8):
            rows = pl.ds(aligned(half * 1024 + b * RES, RES), RES)
            block = kt[:, rows].astype(F32)
            for p in range(PAIRS):
                kn[p, rows, :] = block[p * 2 * HD : (p + 1) * 2 * HD].T.astype(BF)

    turn_keys(core)
    wait_bytes(kt.at[:, there], core_recv.at[0])
    turn_keys(1 - core)
    wait_bytes(vt.at[:, there], core_recv.at[1])
    wait_bytes(qt, kvq_recv.at[2])

    def chunk_of(k):
        far = jnp.where(lax.rem(k, 2) == 1, -((k + 1) // 2), k // 2)
        return lax.rem(z + far + 8, 8)

    def before(k):
        for i in range(1, 8):
            sign, hop = (1, (i + 1) // 2) if i % 2 else (-1, i // 2)

            if i < 3:
                continue

            @pl.when(k == i)
            def _(sign=sign, hop=hop):
                ring_arrived(sign, hop)
                if hop < 4:
                    ring_copy(sign, hop + 1).start()
                else:
                    ring_arrived(-1, 4)

    def out_copy(k):
        to = chunk_of(k)
        return to, remote(o.at[k], out.at[chip], out_send.at[k], out_recv.at[chip], at(to, core))

    def after(k):
        to, copy = out_copy(k)

        @pl.when(to != chip)
        def _():
            copy.start()

        @pl.when(to == chip)
        def _():
            pltpu.make_async_copy(o.at[k], out.at[chip], out_recv.at[chip]).start()

    def rhs_of(chunk, p):
        q = qt[chunk, pl.ds(aligned(p * 64, 64), 64), :]
        none = jnp.zeros((HD, RES), BF)
        return jnp.concatenate(
            [jnp.concatenate([q[:HD], none], 1), jnp.concatenate([none, q[HD:]], 1)], 0
        )

    def score_tile(t, rhs, p, chunk, s, top):
        rows = pl.ds(t * TILE, TILE)
        b = bias[chunk, rows, :].astype(F32)
        scores = jnp.dot(kn[p, rows, :], rhs, preferred_element_type=F32) + jnp.concatenate([b, b], 1)
        s[rows, :] = scores
        return jnp.maximum(top, jnp.max(scores.reshape(TILE // 8, 8, 2 * RES), axis=0))

    def value_tile(t, p, s, top, total, acc):
        rows = pl.ds(t * TILE, TILE)
        e = jnp.exp(s[rows, :] - top)
        total = total + jnp.sum(e.reshape(TILE // 8, 8, 2 * RES), axis=0)
        v = vt[pl.ds(aligned(p * 64, 64), 64), rows]
        return total, acc + jnp.dot(v, e.astype(BF), preferred_element_type=F32)

    lowest = jnp.full((8, 2 * RES), -jnp.inf, F32)
    tiles_n = KEYS // TILE

    def first(s):
        chunk = chunk_of(jnp.int32(0))
        rhs = rhs_of(chunk, jnp.int32(0))
        top = lowest
        for t in range(tiles_n):
            top = score_tile(t, rhs, jnp.int32(0), chunk, s, top)
        return top

    def both(u, v, top, s_now, s_next):
        k, p = u // PAIRS, lax.rem(u, PAIRS)
        kv, pv = v // PAIRS, lax.rem(v, PAIRS)
        chunk = chunk_of(kv)

        @pl.when(jnp.logical_and(pv == 0, v < 8 * PAIRS))
        def _():
            before(kv)

        kv = jnp.minimum(kv, 7)
        chunk = chunk_of(kv)
        top = jnp.max(top, axis=0, keepdims=True)
        rhs = rhs_of(chunk, pv)
        total = jnp.zeros((8, 2 * RES), F32)
        acc = jnp.zeros((2 * HD, 2 * RES), F32)
        top_next = lowest
        for t in range(tiles_n):
            top_next = score_tile(t, rhs, pv, chunk, s_next, top_next)
            total, acc = value_tile(t, p, s_now, top, total, acc)
        result = acc / jnp.sum(total, axis=0, keepdims=True)
        o[k, pl.ds(aligned(p * 64, 64), HD), :] = result[:HD, :RES]
        o[k, pl.ds(aligned(p * 64 + HD, HD), HD), :] = result[HD:, RES:]

        @pl.when(p == PAIRS - 1)
        def _():
            after(k)

        return top_next

    def body(i, top):
        top = both(2 * i, 2 * i + 1, top, sa, sb)
        return both(2 * i + 1, 2 * i + 2, top, sb, sa)

    lax.fori_loop(0, 4 * PAIRS, body, first(sa))

    for h in range(8):
        wait_bytes(out.at[h], out_recv.at[h])
    for k in range(8):
        to, copy = out_copy(jnp.int32(k))

        @pl.when(to != chip)
        def _(copy=copy):
            copy.wait_send()

    for d in range(1, 8):
        tile_copy(d).wait_send()
        for c in kvq_copies(d):
            c.wait_send()

    @pl.when(jnp.logical_not(owner))
    def _():
        tile_copy(0).wait_send()

    @pl.when(owner)
    def _():
        lo_copy.wait_send()

    for c in passed:
        c.wait_send()
    for k in range(1, 5):
        ring_copy(1, k).wait_send()
        ring_copy(-1, k).wait_send()


def attention(qkv, tiles):
    dma = pltpu.SemaphoreType.DMA
    return pl.pallas_call(
        attention_kernel,
        name="attention",
        out_shape=jax.ShapeDtypeStruct((H, ROWS, RES), F32),
        in_specs=[VMEM, VMEM],
        out_specs=VMEM,
        scratch_shapes=[
            pltpu.VMEM((ROWS, KEYS), BF),
            pltpu.VMEM((ROWS, KEYS), BF),
            pltpu.VMEM((8, ROWS, RES), BF),
            pltpu.VMEM((8, KEYS, RES), BF),
            pltpu.VMEM((PAIRS, KEYS, 2 * HD), BF),
            pltpu.VMEM((KEYS, 2 * RES), F32),
            pltpu.VMEM((KEYS, 2 * RES), F32),
            pltpu.VMEM((8, ROWS, RES), F32),
            dma((8,)),
            dma,
            dma((8, 3)),
            dma((2,)),
            dma((2, 4)),
            dma((8,)),
            dma,
            dma((3,)),
            dma((2,)),
            dma((2, 4)),
            dma((8,)),
            dma,
        ],
        compiler_params=pltpu.CompilerParams(
            collective_id=0, has_side_effects=True, vmem_limit_bytes=LIMIT
        ),
    )(qkv, tiles)


def final_kernel(a_ref, gate_ref, w_ref, o_ref):
    w = w_ref[...]
    for s in range(SEQS):
        attended = jnp.concatenate([a_ref[h, s * HD : (s + 1) * HD, :] for h in range(H)], 0)
        gated = (gate_ref[s] * attended).T.astype(BF)
        o_ref[s] = jnp.dot(gated, w, preferred_element_type=F32).astype(BF)


def final(attended, gate, w):
    return pl.pallas_call(
        final_kernel,
        name="final",
        out_shape=jax.ShapeDtypeStruct((SEQS, RES, CH), BF),
        in_specs=[VMEM] * 3,
        out_specs=VMEM,
        compiler_params=pltpu.CompilerParams(vmem_limit_bytes=LIMIT),
    )(attended, gate, w)


def local(x, pair, x_gain, x_shift, pair_gain, wq, wk, wv, wg, gate_shift, w_bias, w_out):
    tiles = pair_bias(pair, pair_gain, w_bias)
    qkv, gate = projections(x, x_gain, x_shift, wk, wv, wq, wg, gate_shift)
    return final(attention(qkv, tiles), gate, w_out)


def solution(mesh):
    split = P("seq", "res", None)
    in_specs = (split, split) + (P(),) * 10
    return jax.shard_map(local, mesh=mesh, in_specs=in_specs, out_specs=split, check_vma=False)
```

time: 523 us -> 127 us (0.24)
  the two profiles are of different devices: /device:TPU:128 before, /device:TPU:7 now
where the time goes in v1:
time: 127 us; the launch traced here: 126 us
  Pallas kernels  125 us (98%)
  local copies, waits for them, and re-layouts  1.46 us (1%)
    pallas_call x1, Pallas kernels, attention(): pl.pallas_call(attention_kernel, name='attention', out_shape=jax.ShapeDty...  108 us
    pallas_call x1, Pallas kernels, pair_bias(): pl.pallas_call(functools.partial(pair_kernel, steps), name='pair_bias', g...  8.91 us
    pallas_call x1, Pallas kernels, projections(): pl.pallas_call(proj_kernel, name='projections', out_shape=(jax.ShapeDtype...  4.63 us
    pallas_call x1, Pallas kernels, final(): pl.pallas_call(final_kernel, name='final', out_shape=jax.ShapeDtypeStruct...  2.95 us

profile of v1, /device:TPU:7, one launch (start us, length us, event | category | flops | bytes accessed | tf_op | source)
XLA Modules:
  0.0 126.3 jit_solution(17511146691144853381)
XLA Ops:
  0.0 1.5 %copy.13.gs_ref = f32[256,1]{1,0:T(8,128)} copy(f32[256,1]{0,1:T(1,128)} %bitcast.6) | data formatting | bytes 2048 | tf_op jit(solution)/shard_map/reshape | solution.py:99
  1.5 8.9 %pair_bias.1.tiles = bf16[8,128,128]{2,1,0:T(8,128)(2,1)} custom-call(bf16[128,128,128]{2,1,0:T(8,128)(2,1)} %x_ref.3, f32[1,128]{1,0:T(1,128)} %bitcast.9, bf16[8,128]{1,0:T(8,128)(2,1)} %bitcast.5), custom_call_target="tpu_custom_call" | custom-call | tf_op jit(solution)/shard_map/pair_bias/pallas_call | solution.py:50
  10.4 4.6 %projections.1 = (bf16[8,3,320,128]{3,2,1,0:T(8,128)(2,1)}, f32[10,256,128]{2,1,0:T(8,128)}) custom-call(bf16[10,128,256]{2,1,0:T(8,128)(2,1)} %x_ref.2, f32[1,256]{1,0:T(1,128)} %bitcast.7, f32[1,256]{1,0:T(1,128)} %bitcast.8, bf16[256,256]{1,0:T(8,128)(2,1)} %wk_ref.1, bf16[256,256]{1,0:T(8,128)(2,1)} %wv_ref.1, bf16[256,256]{1,0:T(8,128)(2,1)} %wq_ref.1, ...), custom_call_target="tpu_custom_call" | custom-call | tf_op jit(solution)/shard_map/projections/pallas_call | solution.py:89
  15.0 108.3 %attention.1.a_ref = f32[8,320,128]{2,1,0:T(8,128)} custom-call(bf16[8,3,320,128]{3,2,1,0:T(8,128)(2,1)} %get-tuple-element.7.qkv, bf16[8,128,128]{2,1,0:T(8,128)(2,1)} %pair_bias.1.tiles), custom_call_target="tpu_custom_call" | custom-call | tf_op jit(solution)/shard_map/attention/pallas_call | solution.py:356
  123.3 2.9 %final.1 = bf16[10,128,256]{2,1,0:T(8,128)(2,1)} custom-call(f32[8,320,128]{2,1,0:T(8,128)} %attention.1.a_ref, f32[10,256,128]{2,1,0:T(8,128)} %get-tuple-element.8.gate_ref, bf16[256,256]{1,0:T(8,128)(2,1)} %w_ref.1), custom_call_target="tpu_custom_call" | custom-call | tf_op jit(solution)/shard_map/final/pallas_call | solution.py:399

commit v2 on v0

v2 whole, which is shorter than its diff:
```python
import jax
import jax.numpy as jnp
from jax import lax
from jax.experimental import pallas as pl
from jax.experimental.pallas import tpu as pltpu
from jax.sharding import PartitionSpec as P

F32, BF = jnp.float32, jnp.bfloat16
MESH = pl.DeviceIdType.MESH
VMEM = pl.BlockSpec(memory_space=pltpu.VMEM)
HBM = pl.BlockSpec(memory_space=pl.ANY)

H, HD = 8, 32
SEQS, RES, CH, CP = 10, 128, 256, 128
KEYS = 2048
ROWS = SEQS * HD
PAIRS = SEQS // 2
PW = 2 * HD
TILE = 256
STEP = 32
LIMIT = 60 * 2**20
RING_AT = ((1, 1, 0), (2, 1, 1), (9, 2, 0), (12, 2, 1), (20, 3, 0), (25, 3, 1), (35, 4, 0))
SEND_AT = {}
GATE_AT = 15
MIDDLE = 2
EARLY = 1


def aligned(value, n):
    return pl.multiple_of(value, n)


def column(row, n):
    return jnp.broadcast_to(row, (n, row.shape[1])).T


def normalize(values, gain):
    mean = jnp.mean(values, axis=0, keepdims=True)
    centered = values - mean
    var = jnp.mean(centered * centered, axis=0, keepdims=True)
    return centered * lax.rsqrt(var + 1e-05) * gain


def kernel(
    x_hbm, pair_hbm, gain_ref, shift_ref, pair_gain_ref, wq_hbm, wk_hbm, wv_hbm, wg_hbm, gs_ref, wb_ref, wo_hbm,
    out,
    pair_v, x_v, w_v, logits, tiles, normed_v, qkv, gate, gate_in, came, bias, kn, sa, sb, o, o_last, back, gated_v,
    pair_in, x_in, w_in,
    tile_send, qkv_send, gate_send, core_send, ring_send, back_send, last_send,
    bias_recv, qkv_recv, gate_recv, core_recv, ring_recv, back_recv, last_recv,
):
    seq, res = lax.axis_index("seq"), lax.axis_index("res")
    z, low = seq // 2, lax.rem(seq, 2)
    chip, core = res // 2, lax.rem(res, 2)
    owner = core == low

    pair_copies = [
        pltpu.make_async_copy(pair_hbm.at[pl.ds(i * STEP, STEP)], pair_v.at[pl.ds(i * STEP, STEP)], pair_in.at[i])
        for i in range(RES // STEP)
    ]
    for c in pair_copies:
        c.start()
    x_copy = pltpu.make_async_copy(x_hbm, x_v, x_in)
    x_copy.start()
    w_copies = [
        pltpu.make_async_copy(w, w_v.at[i], w_in.at[i])
        for i, w in enumerate((wk_hbm, wv_hbm, wq_hbm, wg_hbm, wo_hbm))
    ]
    for c in w_copies:
        c.start()

    def at(other_chip, other_core):
        return (seq, other_chip * 2 + other_core)

    def along_z(d):
        return (lax.rem(z + d + 8, 8) * 2 + low, res)

    sibling = at(chip, 1 - core)

    def remote(src, dst, send, recv, device):
        return pltpu.make_async_remote_copy(
            src_ref=src, dst_ref=dst, send_sem=send, recv_sem=recv, device_id=device, device_id_type=MESH
        )

    def wait_bytes(ref, sem):
        pltpu.make_async_copy(ref, ref, sem).wait()

    barrier = pltpu.get_barrier_semaphore()
    for other in range(2):
        for d in range(other ^ 1, 16):
            peer = (z * 2 + lax.rem(low + other, 2), lax.rem(res + d, 16))
            pl.semaphore_signal(barrier, inc=1, device_id=peer, device_id_type=MESH)
    for sign in (1, -1):
        pl.semaphore_signal(barrier, inc=1, device_id=along_z(sign), device_id_type=MESH)

    def qkv_copy(d, p):
        to = lax.rem(chip + d, 8)
        return remote(qkv.at[to, p], came.at[p, core, chip], qkv_send.at[p, d], qkv_recv.at[p], at(to, core))

    x_gain, x_shift = column(gain_ref[...], 2 * RES), column(shift_ref[...], 2 * RES)
    x_copy.wait()
    for c in w_copies:
        c.wait()
    wt = [w_v[i].astype(F32).T.astype(BF) for i in range(4)]

    def project(p):
        turned = jnp.concatenate([x_v[2 * p].T, x_v[2 * p + 1].T], 1).astype(F32)
        normed = (normalize(turned, x_gain) + x_shift).astype(BF)
        normed_v[p] = normed
        for j in range(3):
            y = jnp.dot(wt[j], normed, preferred_element_type=F32)
            if j == 2:
                y = y * HD ** (-0.5)
            y = y.astype(BF)
            for h in range(H):
                for s in range(2):
                    qkv[h, p, j, s * HD : (s + 1) * HD, :] = y[h * HD : (h + 1) * HD, s * RES : (s + 1) * RES]

    def send_pair(p):
        pltpu.make_async_copy(qkv.at[chip, p], came.at[p, core, chip], qkv_recv.at[p]).start()
        for d in range(1, 8):
            qkv_copy(d, p).start()

    pl.semaphore_wait(barrier, 33)
    for p in range(EARLY):
        project(p)
        send_pair(p)

    pair_gain = column(pair_gain_ref[...], RES)
    pair_gain = jnp.concatenate([pair_gain, pair_gain], 1)
    wb = wb_ref[...]

    def pair_step(i, carry):
        rows = pl.ds(i * STEP, STEP)
        pltpu.make_async_copy(pair_hbm.at[rows], pair_v.at[rows], pair_in.at[i]).wait()
        for j in range(STEP // 2):
            row = i * STEP + 2 * j
            turned = jnp.concatenate([pair_v[row].T, pair_v[row + 1].T], 1).astype(F32)
            y = jnp.dot(wb, normalize(turned, pair_gain).astype(BF), preferred_element_type=F32)
            row = aligned(row * H, 2 * H)
            logits[pl.ds(row, H), :] = y[:, :RES]
            logits[pl.ds(row + H, H), :] = y[:, RES:]
        return carry

    lax.fori_loop(0, RES // STEP, pair_step, 0)
    for h in range(H):
        tiles[h] = logits[pl.ds(h, RES, stride=H), :].T.astype(BF)

    mine = pl.ds(aligned(core * 1024 + chip * RES, RES), RES)

    def tile_copy(d, other):
        to = lax.rem(chip + d, 8)
        device = (z * 2 + lax.rem(low + other, 2), to * 2 + low)
        return remote(tiles.at[to], bias.at[z, mine, :], tile_send.at[other, d], bias_recv, device)

    @pl.when(owner)
    def _():
        pltpu.make_async_copy(tiles.at[chip], bias.at[z, mine, :], bias_recv).start()

    @pl.when(jnp.logical_not(owner))
    def _():
        tile_copy(0, 0).start()

    tile_copy(0, 1).start()
    for d in range(1, 8):
        for other in range(2):
            tile_copy(d, other).start()

    def half_of(chunk, half):
        return bias.at[chunk, pl.ds(half * (KEYS // 2), KEYS // 2), :]

    def ring_copy(sign, k, half):
        i = 0 if sign > 0 else 1
        ref = half_of(lax.rem(z - sign * (k - 1) + 8, 8), half)
        return remote(ref, ref, ring_send.at[i, k - 1, half], ring_recv.at[i, k - 1, half], along_z(sign))

    def ring_arrived(sign, k, half):
        ref = half_of(lax.rem(z - sign * k + 8, 8), half)
        wait_bytes(ref, ring_recv.at[0 if sign > 0 else 1, k - 1, half])

    def goes(sign, k, half):
        return k < 4 or (k == 4 and half == (0 if sign > 0 else 1))

    def take(sign, k, half):
        if goes(sign, k, half):
            ring_arrived(sign, k, half)
        if goes(sign, k + 1, half):
            ring_copy(sign, k + 1, half).start()

    for p in range(EARLY, PAIRS):
        project(p)
        if p == MIDDLE:
            wait_bytes(bias.at[z], bias_recv)
            for half in range(2):
                for sign in (1, -1):
                    ring_copy(sign, 1, half).start()
        if p not in SEND_AT.values():
            send_pair(p)

    gate_shift = column(gs_ref[...], 2 * RES)
    for p in range(PAIRS):
        g = jax.nn.sigmoid(jnp.dot(wt[3], normed_v[p], preferred_element_type=F32) + gate_shift)
        for h in range(H):
            for s in range(2):
                gate[h, (2 * p + s) * HD : (2 * p + s + 1) * HD, :] = g[
                    h * HD : (h + 1) * HD, s * RES : (s + 1) * RES
                ]

    last = lax.rem(z + 4, 8)

    def gate_copy(d):
        to = lax.rem(chip + d, 8)
        return remote(gate.at[to], gate_in, gate_send.at[d], gate_recv, at(to, core))

    def send_gate():
        pltpu.make_async_copy(gate.at[chip], gate_in, gate_recv).start()
        for d in range(1, 8):
            gate_copy(d).start()

    def core_copy(p):
        ref = came.at[p, core, :, pl.ds(0, 2)]
        return remote(ref, ref, core_send.at[p], core_recv.at[p], sibling)

    def turn_keys(p, half):
        for b in range(8):
            rows = pl.ds(aligned(half * 1024 + b * RES, RES), RES)
            kn[p, rows, :] = came[p, half, b, 0].astype(F32).T.astype(BF)

    def pair_arrived(p):
        wait_bytes(came.at[p, core], qkv_recv.at[p])
        core_copy(p).start()
        turn_keys(p, core)
        wait_bytes(came.at[p, 1 - core, :, pl.ds(0, 2)], core_recv.at[p])
        turn_keys(p, 1 - core)

    def chunk_of(k):
        far = jnp.where(lax.rem(k, 2) == 1, -((k + 1) // 2), k // 2)
        return lax.rem(z + far + 8, 8)

    def place(v):
        w = v - 15
        k = jnp.where(v < 9, v // 3, jnp.where(v < 15, lax.rem(v, 3), 3 + w // PAIRS))
        p = jnp.where(v < 9, lax.rem(v, 3), jnp.where(v < 15, v // 3, lax.rem(v, PAIRS)))
        return k, p

    def before(v):
        k, p = place(v)

        for unit, hop, half in RING_AT:

            @pl.when(v == unit)
            def _(hop=hop, half=half):
                for sign in (1, -1):
                    take(sign, hop, half)
                    if hop == 4:
                        take(sign, hop, 1)

        @pl.when(jnp.logical_and(v == GATE_AT, chip == last))
        def _():
            send_gate()

        @pl.when(jnp.logical_and(k == 0, v < 15))
        def _():
            pair_arrived(p)

        for unit, pair in SEND_AT.items():

            @pl.when(v == unit)
            def _(pair=pair):
                send_pair(pair)

    def after(k, p):
        to = chunk_of(k)
        rows = pl.ds(aligned(p * PW, PW), PW)

        def send(src, dst, send_sem, recv_sem):
            @pl.when(to != chip)
            def _():
                remote(src, dst, send_sem, recv_sem, at(to, core)).start()

            @pl.when(to == chip)
            def _():
                pltpu.make_async_copy(src, dst, recv_sem).start()

        @pl.when(k < 7)
        def _():
            send(o.at[k, rows, :], back.at[chip, rows, :], back_send, back_recv)

        @pl.when(k == 7)
        def _():
            send(o_last.at[rows, :], gated_v.at[chip, rows, :], last_send, last_recv)

    def rhs_of(chunk, p):
        q = came[p, core, chunk, 2]
        none = jnp.zeros((HD, RES), BF)
        return jnp.concatenate([jnp.concatenate([q[:HD], none], 1), jnp.concatenate([none, q[HD:]], 1)], 0)

    def score_tile(t, rhs, p, chunk, s, top):
        rows = pl.ds(t * TILE, TILE)
        b = bias[chunk, rows, :].astype(F32)
        scores = jnp.dot(kn[p, rows, :], rhs, preferred_element_type=F32) + jnp.concatenate([b, b], 1)
        s[rows, :] = scores
        return jnp.maximum(top, jnp.max(scores.reshape(TILE // 8, 8, 2 * RES), axis=0))

    def value_tile(t, p, s, top, total, acc):
        e = jnp.exp(s[pl.ds(t * TILE, TILE), :] - top)
        total = total + jnp.sum(e.reshape(TILE // 8, 8, 2 * RES), axis=0)
        v = [came[p, (t * TILE) // 1024, (t * TILE) % 1024 // RES + i, 1] for i in range(TILE // RES)]
        return total, acc + jnp.dot(jnp.concatenate(v, 1), e.astype(BF), preferred_element_type=F32)

    lowest = jnp.full((8, 2 * RES), -jnp.inf, F32)
    steps = KEYS // TILE
    units = 8 * PAIRS

    def first(s):
        zero = jnp.int32(0)
        before(zero)
        rhs = rhs_of(z, zero)
        top = lowest
        for t in range(steps):
            top = score_tile(t, rhs, zero, z, s, top)
        return top

    def both(u, top, s_now, s_next):
        before(u + 1)
        k, p = place(u)
        kv, pv = place(jnp.minimum(u + 1, units - 1))
        chunk = chunk_of(kv)
        top = jnp.max(top, axis=0, keepdims=True)
        rhs = rhs_of(chunk, pv)
        total = jnp.zeros((8, 2 * RES), F32)
        acc = jnp.zeros((PW, 2 * RES), F32)
        top_next = lowest
        for t in range(steps):
            top_next = score_tile(t, rhs, pv, chunk, s_next, top_next)
            total, acc = value_tile(t, p, s_now, top, total, acc)
        result = acc / jnp.sum(total, axis=0, keepdims=True)
        halves = (result[:HD, :RES], result[HD:, RES:])

        @pl.when(k < 7)
        def _():
            for i, half in enumerate(halves):
                o[k, pl.ds(aligned(p * PW + i * HD, HD), HD), :] = half

        @pl.when(k == 7)
        def _():
            @pl.when(p == 0)
            def _():
                wait_bytes(gate_in, gate_recv)

            for i, half in enumerate(halves):
                rows = pl.ds(aligned(p * PW + i * HD, HD), HD)
                o_last[rows, :] = (gate_in[rows, :] * half).astype(BF)

        after(k, p)
        return top_next

    def body(i, top):
        top = both(2 * i, top, sa, sb)
        return both(2 * i + 1, top, sb, sa)

    lax.fori_loop(0, units // 2, body, first(sa))

    @pl.when(chip != last)
    def _():
        wait_bytes(back, back_recv)
        for h in range(H):
            gated_v[h] = (gate[h] * back[h]).astype(BF)

    @pl.when(chip == last)
    def _():
        wait_bytes(gated_v, last_recv)

    wo = w_v[4]
    for s in range(SEQS):
        gated = jnp.concatenate([gated_v[h, s * HD : (s + 1) * HD, :] for h in range(H)], 0)
        out[s] = jnp.dot(gated.T, wo, preferred_element_type=F32).astype(BF)

    @pl.when(chip != last)
    def _():
        wait_bytes(o.at[pl.ds(0, 6)], back_send)
        wait_bytes(o_last, last_send)

    @pl.when(chip == last)
    def _():
        wait_bytes(o.at[pl.ds(0, 7)], back_send)
        for d in range(1, 8):
            gate_copy(d).wait_send()
    for d in range(8):
        tile_copy(d, 1).wait_send()
        if d:
            tile_copy(d, 0).wait_send()

    @pl.when(jnp.logical_not(owner))
    def _():
        tile_copy(0, 0).wait_send()

    for p in range(PAIRS):
        for d in range(1, 8):
            qkv_copy(d, p).wait_send()
        core_copy(p).wait_send()
    for sign in (1, -1):
        for half in range(2):
            for k in range(1, 5):
                if goes(sign, k, half):
                    ring_copy(sign, k, half).wait_send()


def local(x, pair, x_gain, x_shift, pair_gain, wq, wk, wv, wg, gate_shift, w_bias, w_out):
    dma = pltpu.SemaphoreType.DMA
    return pl.pallas_call(
        kernel,
        name="attention",
        out_shape=jax.ShapeDtypeStruct((SEQS, RES, CH), BF),
        in_specs=[HBM, HBM, VMEM, VMEM, VMEM, HBM, HBM, HBM, HBM, VMEM, VMEM, HBM],
        out_specs=VMEM,
        scratch_shapes=[
            pltpu.VMEM((RES, RES, CP), BF),
            pltpu.VMEM((SEQS, RES, CH), BF),
            pltpu.VMEM((5, CH, CH), BF),
            pltpu.VMEM((RES * H, RES), F32),
            pltpu.VMEM((H, RES, RES), BF),
            pltpu.VMEM((PAIRS, CH, 2 * RES), BF),
            pltpu.VMEM((H, PAIRS, 3, PW, RES), BF),
            pltpu.VMEM((H, ROWS, RES), F32),
            pltpu.VMEM((ROWS, RES), F32),
            pltpu.VMEM((PAIRS, 2, 8, 3, PW, RES), BF),
            pltpu.VMEM((8, KEYS, RES), BF),
            pltpu.VMEM((PAIRS, KEYS, PW), BF),
            pltpu.VMEM((KEYS, 2 * RES), F32),
            pltpu.VMEM((KEYS, 2 * RES), F32),
            pltpu.VMEM((7, ROWS, RES), F32),
            pltpu.VMEM((ROWS, RES), BF),
            pltpu.VMEM((8, ROWS, RES), F32),
            pltpu.VMEM((8, ROWS, RES), BF),
            dma((RES // STEP,)),
            dma,
            dma((5,)),
            dma((2, 8)),
            dma((PAIRS, 8)),
            dma((8,)),
            dma((PAIRS,)),
            dma((2, 4, 2)),
            dma,
            dma,
            dma,
            dma((PAIRS,)),
            dma,
            dma((PAIRS,)),
            dma((2, 4, 2)),
            dma,
            dma,
        ],
        compiler_params=pltpu.CompilerParams(
            collective_id=0, has_side_effects=True, vmem_limit_bytes=LIMIT
        ),
    )(
        x, pair, x_gain.reshape(1, CH), x_shift.reshape(1, CH), pair_gain.reshape(1, CP),
        wq, wk, wv, wg, gate_shift.reshape(1, CH), w_bias.T, w_out,
    )


def solution(mesh):
    split = P("seq", "res", None)
    in_specs = (split, split) + (P(),) * 10
    return jax.shard_map(local, mesh=mesh, in_specs=in_specs, out_specs=split, check_vma=False)
```

time: 523 us -> 89.7 us (0.17)
  the two profiles are of different devices: /device:TPU:128 before, /device:TPU:7 now
where the time goes in v2:
time: 89.7 us; the launch traced here: 89.6 us
  Pallas kernels  87.6 us (98%)
  local copies, waits for them, and re-layouts  1.97 us (2%)
    pallas_call x1, Pallas kernels, local(): pl.pallas_call(kernel, name='attention', out_shape=jax.ShapeDtypeStruct((...  87.6 us
    unnamed x1, local copies, waits for them, and re-layouts  1.97 us

profile of v2, /device:TPU:7, one launch (start us, length us, event | category | flops | bytes accessed | tf_op | source)
XLA Modules:
  0.0 89.6 jit_solution(9771037775452931236)
XLA Ops:
  0.0 87.6 %attention.1 = bf16[10,128,256]{2,1,0:T(8,128)(2,1)} custom-call(bf16[10,128,256]{2,1,0:T(8,128)(2,1)} %x_hbm.1, bf16[128,128,128]{2,1,0:T(8,128)(2,1)} %pair_hbm.1, f32[1,256]{1,0:T(1,128)} %bitcast.6, f32[1,256]{1,0:T(1,128)} %bitcast.7, f32[1,128]{1,0:T(1,128)} %bitcast.9, bf16[256,256]{1,0:T(8,128)(2,1)} %wq_hbm.1, bf16[256,256]{1,0:T(8,128)(2,1)} %wk_hbm.1, ...), custom_call_target="tpu_custom_call" | custom-call | tf_op jit(solution)/shard_map/attention/pallas_call | solution.py:411
  87.6 2.0 %copy.14 = bf16[10,128,256]{2,1,0:T(8,128)(2,1)} copy(bf16[10,128,256]{2,1,0:T(8,128)(2,1)} %attention.1) | data formatting | bytes 1310720

commit v3 on v2

--- a/solution.py
+++ b/solution.py
@@ -17,13 +17,13 @@
 PAIRS = SEQS // 2
 PW = 2 * HD
 TILE = 256
-STEP = 32
+HALF = RES // 2
+STEP = 16
 LIMIT = 60 * 2**20
 RING_AT = ((1, 1, 0), (2, 1, 1), (9, 2, 0), (12, 2, 1), (20, 3, 0), (25, 3, 1), (35, 4, 0))
 SEND_AT = {}
-GATE_AT = 15
-MIDDLE = 2
-EARLY = 1
+GATE_AT = 9
+START_AT = (0, 1)
 
 
 def aligned(value, n):
@@ -54,12 +54,13 @@
     chip, core = res // 2, lax.rem(res, 2)
     owner = core == low
 
-    pair_copies = [
-        pltpu.make_async_copy(pair_hbm.at[pl.ds(i * STEP, STEP)], pair_v.at[pl.ds(i * STEP, STEP)], pair_in.at[i])
-        for i in range(RES // STEP)
-    ]
-    for c in pair_copies:
-        c.start()
+    def pair_copy(half, i):
+        rows, keys = pl.ds(i * STEP, STEP), pl.ds(half * HALF, HALF)
+        return pltpu.make_async_copy(pair_hbm.at[rows, keys], pair_v.at[rows, keys], pair_in.at[half, i])
+
+    for half in range(2):
+        for i in range(RES // STEP):
+            pair_copy(half, i).start()
     x_copy = pltpu.make_async_copy(x_hbm, x_v, x_in)
     x_copy.start()
     w_copies = [
@@ -92,6 +93,84 @@
             pl.semaphore_signal(barrier, inc=1, device_id=peer, device_id_type=MESH)
     for sign in (1, -1):
         pl.semaphore_signal(barrier, inc=1, device_id=along_z(sign), device_id_type=MESH)
+
+    pair_gain = column(pair_gain_ref[...], RES)
+    pair_gain = jnp.concatenate([pair_gain, pair_gain], 1)
+    wb = wb_ref[...]
+
+    mine = pl.ds(aligned((core * 8 + chip) * HALF, HALF), HALF)
+
+    def logits_of(half):
+        keys = slice(half * HALF, (half + 1) * HALF)
+
+        def pair_step(i, carry):
+            pair_copy(half, i).wait()
+            pair_copy(half, i + RES // STEP // 2).wait()
+            for j in range(STEP // 2):
+                row = i * STEP + 2 * j
+                blocks = [
+                    jnp.concatenate([pair_v[row + k, keys, :], pair_v[row + k + HALF, keys, :]], 0).T
+                    for k in range(2)
+                ]
+                turned = jnp.concatenate(blocks, 1).astype(F32)
+                y = jnp.dot(wb, normalize(turned, pair_gain).astype(BF), preferred_element_type=F32)
+                at_row = aligned(row * H, 2 * H)
+                logits[pl.ds(at_row, H), :] = y[:, :RES]
+                logits[pl.ds(at_row + H, H), :] = y[:, RES:]
+            return carry
+
+        lax.fori_loop(0, RES // STEP // 2, pair_step, 0)
+        for h in range(H):
+            t = logits[pl.ds(h, HALF, stride=H), :].T
+            tiles[half, h] = jnp.concatenate([t[:HALF], t[HALF:]], 1).astype(BF)
+
+    def tile_copy(half, d, other):
+        to = lax.rem(chip + d, 8)
+        device = (z * 2 + lax.rem(low + other, 2), to * 2 + low)
+        return remote(
+            tiles.at[half, to], bias.at[z, half, mine, :], tile_send.at[half, other, d], bias_recv.at[half], device
+        )
+
+    def send_tiles(half):
+        @pl.when(owner)
+        def _():
+            pltpu.make_async_copy(tiles.at[half, chip], bias.at[z, half, mine, :], bias_recv.at[half]).start()
+
+        @pl.when(jnp.logical_not(owner))
+        def _():
+            tile_copy(half, 0, 0).start()
+
+        tile_copy(half, 0, 1).start()
+        for d in range(1, 8):
+            for other in range(2):
+                tile_copy(half, d, other).start()
+
+    logits_of(0)
+    pl.semaphore_wait(barrier, 33)
+    send_tiles(0)
+    logits_of(1)
+    send_tiles(1)
+
+    def half_of(chunk, half):
+        return bias.at[chunk, half]
+
+    def ring_copy(sign, k, half):
+        i = 0 if sign > 0 else 1
+        ref = half_of(lax.rem(z - sign * (k - 1) + 8, 8), half)
+        return remote(ref, ref, ring_send.at[i, k - 1, half], ring_recv.at[i, k - 1, half], along_z(sign))
+
+    def ring_arrived(sign, k, half):
+        ref = half_of(lax.rem(z - sign * k + 8, 8), half)
+        wait_bytes(ref, ring_recv.at[0 if sign > 0 else 1, k - 1, half])
+
+    def goes(sign, k, half):
+        return k < 4 or (k == 4 and half == (0 if sign > 0 else 1))
+
+    def take(sign, k, half):
+        if goes(sign, k, half):
+            ring_arrived(sign, k, half)
+        if goes(sign, k + 1, half):
+            ring_copy(sign, k + 1, half).start()
 
     def qkv_copy(d, p):
         to = lax.rem(chip + d, 8)
@@ -121,77 +200,11 @@
         for d in range(1, 8):
             qkv_copy(d, p).start()
 
-    pl.semaphore_wait(barrier, 33)
-    for p in range(EARLY):
+    for p in range(PAIRS):
         project(p)
-        send_pair(p)
-
-    pair_gain = column(pair_gain_ref[...], RES)
-    pair_gain = jnp.concatenate([pair_gain, pair_gain], 1)
-    wb = wb_ref[...]
-
-    def pair_step(i, carry):
-        rows = pl.ds(i * STEP, STEP)
-        pltpu.make_async_copy(pair_hbm.at[rows], pair_v.at[rows], pair_in.at[i]).wait()
-        for j in range(STEP // 2):
-            row = i * STEP + 2 * j
-            turned = jnp.concatenate([pair_v[row].T, pair_v[row + 1].T], 1).astype(F32)
-            y = jnp.dot(wb, normalize(turned, pair_gain).astype(BF), preferred_element_type=F32)
-            row = aligned(row * H, 2 * H)
-            logits[pl.ds(row, H), :] = y[:, :RES]
-            logits[pl.ds(row + H, H), :] = y[:, RES:]
-        return carry
-
-    lax.fori_loop(0, RES // STEP, pair_step, 0)
-    for h in range(H):
-        tiles[h] = logits[pl.ds(h, RES, stride=H), :].T.astype(BF)
-
-    mine = pl.ds(aligned(core * 1024 + chip * RES, RES), RES)
-
-    def tile_copy(d, other):
-        to = lax.rem(chip + d, 8)
-        device = (z * 2 + lax.rem(low + other, 2), to * 2 + low)
-        return remote(tiles.at[to], bias.at[z, mine, :], tile_send.at[other, d], bias_recv, device)
-
-    @pl.when(owner)
-    def _():
-        pltpu.make_async_copy(tiles.at[chip], bias.at[z, mine, :], bias_recv).start()
-
-    @pl.when(jnp.logical_not(owner))
-    def _():
-        tile_copy(0, 0).start()
-
-    tile_copy(0, 1).start()
-    for d in range(1, 8):
-        for other in range(2):
-            tile_copy(d, other).start()
-
-    def half_of(chunk, half):
-        return bias.at[chunk, pl.ds(half * (KEYS // 2), KEYS // 2), :]
-
-    def ring_copy(sign, k, half):
-        i = 0 if sign > 0 else 1
-        ref = half_of(lax.rem(z - sign * (k - 1) + 8, 8), half)
-        return remote(ref, ref, ring_send.at[i, k - 1, half], ring_recv.at[i, k - 1, half], along_z(sign))
-
-    def ring_arrived(sign, k, half):
-        ref = half_of(lax.rem(z - sign * k + 8, 8), half)
-        wait_bytes(ref, ring_recv.at[0 if sign > 0 else 1, k - 1, half])
-
-    def goes(sign, k, half):
-        return k < 4 or (k == 4 and half == (0 if sign > 0 else 1))
-
-    def take(sign, k, half):
-        if goes(sign, k, half):
-            ring_arrived(sign, k, half)
-        if goes(sign, k + 1, half):
-            ring_copy(sign, k + 1, half).start()
-
-    for p in range(EARLY, PAIRS):
-        project(p)
-        if p == MIDDLE:
-            wait_bytes(bias.at[z], bias_recv)
-            for half in range(2):
+        for half in range(2):
+            if p == START_AT[half]:
+                wait_bytes(half_of(z, half), bias_recv.at[half])
                 for sign in (1, -1):
                     ring_copy(sign, 1, half).start()
         if p not in SEND_AT.values():
@@ -297,7 +310,14 @@
 
     def score_tile(t, rhs, p, chunk, s, top):
         rows = pl.ds(t * TILE, TILE)
-        b = bias[chunk, rows, :].astype(F32)
+        b = jnp.concatenate(
+            [
+                bias[chunk, half, pl.ds((t * TILE // RES + i) * HALF, HALF), :]
+                for i in range(TILE // RES)
+                for half in range(2)
+            ],
+            0,
+        ).astype(F32)
         scores = jnp.dot(kn[p, rows, :], rhs, preferred_element_type=F32) + jnp.concatenate([b, b], 1)
         s[rows, :] = scores
         return jnp.maximum(top, jnp.max(scores.reshape(TILE // 8, 8, 2 * RES), axis=0))
@@ -386,14 +406,15 @@
         wait_bytes(o.at[pl.ds(0, 7)], back_send)
         for d in range(1, 8):
             gate_copy(d).wait_send()
-    for d in range(8):
-        tile_copy(d, 1).wait_send()
-        if d:
-            tile_copy(d, 0).wait_send()
-
-    @pl.when(jnp.logical_not(owner))
-    def _():
-        tile_copy(0, 0).wait_send()
+    for half in range(2):
+        for d in range(8):
+            tile_copy(half, d, 1).wait_send()
+            if d:
+                tile_copy(half, d, 0).wait_send()
+
+        @pl.when(jnp.logical_not(owner))
+        def _(half=half):
+            tile_copy(half, 0, 0).wait_send()
 
     for p in range(PAIRS):
         for d in range(1, 8):
@@ -418,14 +439,14 @@
             pltpu.VMEM((RES, RES, CP), BF),
             pltpu.VMEM((SEQS, RES, CH), BF),
             pltpu.VMEM((5, CH, CH), BF),
-            pltpu.VMEM((RES * H, RES), F32),
-            pltpu.VMEM((H, RES, RES), BF),
+            pltpu.VMEM((HALF * H, RES), F32),
+            pltpu.VMEM((2, H, HALF, RES), BF),
             pltpu.VMEM((PAIRS, CH, 2 * RES), BF),
             pltpu.VMEM((H, PAIRS, 3, PW, RES), BF),
             pltpu.VMEM((H, ROWS, RES), F32),
             pltpu.VMEM((ROWS, RES), F32),
             pltpu.VMEM((PAIRS, 2, 8, 3, PW, RES), BF),
-            pltpu.VMEM((8, KEYS, RES), BF),
+            pltpu.VMEM((8, 2, KEYS // 2, RES), BF),
             pltpu.VMEM((PAIRS, KEYS, PW), BF),
             pltpu.VMEM((KEYS, 2 * RES), F32),
             pltpu.VMEM((KEYS, 2 * RES), F32),
@@ -433,17 +454,17 @@
             pltpu.VMEM((ROWS, RES), BF),
             pltpu.VMEM((8, ROWS, RES), F32),
             pltpu.VMEM((8, ROWS, RES), BF),
-            dma((RES // STEP,)),
+            dma((2, RES // STEP)),
             dma,
             dma((5,)),
-            dma((2, 8)),
+            dma((2, 2, 8)),
             dma((PAIRS, 8)),
             dma((8,)),
             dma((PAIRS,)),
             dma((2, 4, 2)),
             dma,
             dma,
-            dma,
+            dma((2,)),
             dma((PAIRS,)),
             dma,
             dma((PAIRS,)),

time: 89.7 us -> 80.8 us (0.901)
  the two profiles are of different devices: /device:TPU:7 before, /device:TPU:128 now
where the time goes in v3:
time: 80.8 us; the launch traced here: 80.7 us
  Pallas kernels  78.7 us (97%)
  local copies, waits for them, and re-layouts  1.97 us (2%)
    pallas_call x1, Pallas kernels, local(): pl.pallas_call(kernel, name='attention', out_shape=jax.ShapeDtypeStruct((...  78.7 us
    unnamed x1, local copies, waits for them, and re-layouts  1.97 us

profile of v3, /device:TPU:128, one launch (start us, length us, event | category | flops | bytes accessed | tf_op | source)
XLA Modules:
  0.0 80.7 jit_solution(9568764613520262760)
XLA Ops:
  0.0 78.7 %attention.1 = bf16[10,128,256]{2,1,0:T(8,128)(2,1)} custom-call(bf16[10,128,256]{2,1,0:T(8,128)(2,1)} %x_hbm.1, bf16[128,128,128]{2,1,0:T(8,128)(2,1)} %pair_hbm.1, f32[1,256]{1,0:T(1,128)} %bitcast.6, f32[1,256]{1,0:T(1,128)} %bitcast.7, f32[1,128]{1,0:T(1,128)} %bitcast.9, bf16[256,256]{1,0:T(8,128)(2,1)} %wq_hbm.1, bf16[256,256]{1,0:T(8,128)(2,1)} %wk_hbm.1, ...), custom_call_target="tpu_custom_call" | custom-call | tf_op jit(solution)/shard_map/attention/pallas_call | solution.py:432
  78.7 2.0 %copy.14 = bf16[10,128,256]{2,1,0:T(8,128)(2,1)} copy(bf16[10,128,256]{2,1,0:T(8,128)(2,1)} %attention.1) | data formatting | bytes 1310720

commit v4 on v3

--- a/solution.py
+++ b/solution.py
@@ -257,6 +257,11 @@
         return k, p
 
     def before(v):
+        @pl.when(jnp.logical_or(v < 15, lax.rem(v, PAIRS) == 0))
+        def _():
+            before_some(v)
+
+    def before_some(v):
         k, p = place(v)
 
         for unit, hop, half in RING_AT:
@@ -282,7 +287,7 @@
             def _(pair=pair):
                 send_pair(pair)
 
-    def after(k, p):
+    def after(k, p, halves):
         to = chunk_of(k)
         rows = pl.ds(aligned(p * PW, PW), PW)
 
@@ -297,10 +302,19 @@
 
         @pl.when(k < 7)
         def _():
+            for i, half in enumerate(halves):
+                o[k, pl.ds(aligned(p * PW + i * HD, HD), HD), :] = half
             send(o.at[k, rows, :], back.at[chip, rows, :], back_send, back_recv)
 
         @pl.when(k == 7)
         def _():
+            @pl.when(p == 0)
+            def _():
+                wait_bytes(gate_in, gate_recv)
+
+            for i, half in enumerate(halves):
+                part = pl.ds(aligned(p * PW + i * HD, HD), HD)
+                o_last[part, :] = (gate_in[part, :] * half).astype(BF)
             send(o_last.at[rows, :], gated_v.at[chip, rows, :], last_send, last_recv)
 
     def rhs_of(chunk, p):
@@ -355,24 +369,7 @@
             top_next = score_tile(t, rhs, pv, chunk, s_next, top_next)
             total, acc = value_tile(t, p, s_now, top, total, acc)
         result = acc / jnp.sum(total, axis=0, keepdims=True)
-        halves = (result[:HD, :RES], result[HD:, RES:])
-
-        @pl.when(k < 7)
-        def _():
-            for i, half in enumerate(halves):
-                o[k, pl.ds(aligned(p * PW + i * HD, HD), HD), :] = half
-
-        @pl.when(k == 7)
-        def _():
-            @pl.when(p == 0)
-            def _():
-                wait_bytes(gate_in, gate_recv)
-
-            for i, half in enumerate(halves):
-                rows = pl.ds(aligned(p * PW + i * HD, HD), HD)
-                o_last[rows, :] = (gate_in[rows, :] * half).astype(BF)
-
-        after(k, p)
+        after(k, p, (result[:HD, :RES], result[HD:, RES:]))
         return top_next
 
     def body(i, top):

time: 80.8 us -> 79.3 us (0.981); the launches traced: 80.7 us -> 77.7 us
  Pallas kernels: 78.7 us -> 75.8 us
    pallas_call x1, Pallas kernels: 78.7 us -> 75.8 us  [local(): pl.pallas_call(kernel, name='attention', out_shape=jax.ShapeDtypeStruct((...]
where the time goes in v4:
time: 79.3 us; the launch traced here: 77.7 us
  Pallas kernels  75.8 us (96%)
  local copies, waits for them, and re-layouts  1.97 us (2%)
    pallas_call x1, Pallas kernels, local(): pl.pallas_call(kernel, name='attention', out_shape=jax.ShapeDtypeStruct((...  75.8 us
    unnamed x1, local copies, waits for them, and re-layouts  1.97 us

profile of v4, /device:TPU:128, one launch (start us, length us, event | category | flops | bytes accessed | tf_op | source)
XLA Modules:
  0.0 77.7 jit_solution(6378240686865853739)
XLA Ops:
  0.0 75.8 %attention.1 = bf16[10,128,256]{2,1,0:T(8,128)(2,1)} custom-call(bf16[10,128,256]{2,1,0:T(8,128)(2,1)} %x_hbm.1, bf16[128,128,128]{2,1,0:T(8,128)(2,1)} %pair_hbm.1, f32[1,256]{1,0:T(1,128)} %bitcast.6, f32[1,256]{1,0:T(1,128)} %bitcast.7, f32[1,128]{1,0:T(1,128)} %bitcast.9, bf16[256,256]{1,0:T(8,128)(2,1)} %wq_hbm.1, bf16[256,256]{1,0:T(8,128)(2,1)} %wk_hbm.1, ...), custom_call_target="tpu_custom_call" | custom-call | tf_op jit(solution)/shard_map/attention/pallas_call | solution.py:429
  75.8 2.0 %copy.14 = bf16[10,128,256]{2,1,0:T(8,128)(2,1)} copy(bf16[10,128,256]{2,1,0:T(8,128)(2,1)} %attention.1) | data formatting | bytes 1310720

commit v5 on v4

--- a/solution.py
+++ b/solution.py
@@ -246,9 +246,11 @@
         wait_bytes(came.at[p, 1 - core, :, pl.ds(0, 2)], core_recv.at[p])
         turn_keys(p, 1 - core)
 
+    side = 1 - 2 * lax.rem(chip, 2)
+
     def chunk_of(k):
         far = jnp.where(lax.rem(k, 2) == 1, -((k + 1) // 2), k // 2)
-        return lax.rem(z + far + 8, 8)
+        return lax.rem(z + side * far + 8, 8)
 
     def place(v):
         w = v - 15

time: 79.3 us -> 78 us (0.984); the launches traced: 77.7 us -> 77.8 us
  no operation moved by 1% of the time
where the time goes in v5:
time: 78 us; the launch traced here: 77.8 us
  Pallas kernels  75.8 us (97%)
  local copies, waits for them, and re-layouts  1.97 us (3%)
    pallas_call x1, Pallas kernels, local(): pl.pallas_call(kernel, name='attention', out_shape=jax.ShapeDtypeStruct((...  75.8 us
    unnamed x1, local copies, waits for them, and re-layouts  1.97 us

profile of v5, /device:TPU:128, one launch (start us, length us, event | category | flops | bytes accessed | tf_op | source)
XLA Modules:
  0.0 77.8 jit_solution(14909538890326781945)
XLA Ops:
  0.0 75.8 %attention.1 = bf16[10,128,256]{2,1,0:T(8,128)(2,1)} custom-call(bf16[10,128,256]{2,1,0:T(8,128)(2,1)} %x_hbm.1, bf16[128,128,128]{2,1,0:T(8,128)(2,1)} %pair_hbm.1, f32[1,256]{1,0:T(1,128)} %bitcast.6, f32[1,256]{1,0:T(1,128)} %bitcast.7, f32[1,128]{1,0:T(1,128)} %bitcast.9, bf16[256,256]{1,0:T(8,128)(2,1)} %wq_hbm.1, bf16[256,256]{1,0:T(8,128)(2,1)} %wk_hbm.1, ...), custom_call_target="tpu_custom_call" | custom-call | tf_op jit(solution)/shard_map/attention/pallas_call | solution.py:431
  75.9 2.0 %copy.14 = bf16[10,128,256]{2,1,0:T(8,128)(2,1)} copy(bf16[10,128,256]{2,1,0:T(8,128)(2,1)} %attention.1) | data formatting | bytes 1310720
